TPU v7x, 256 devices: a whole 4x4x8 slice. The times are simulated.
256 devices in a mesh: dp: 64 (over z_lo, y, x), mp: 4 (over z_hi, core).
Axes of the slice: x: 4, y: 4, z: 8 (z_hi: 2, z_lo: 4; z = z_hi * 4 + z_lo), core: 2. Of those that a mesh axis runs over, the one named last changes fastest.
Arguments:
- tokens: bfloat16 [16384, 8192], P('dp', 'mp'), may hold values from -8 to 8
- attn_gain: bfloat16 [8192], replicated, may hold values from 0.5 to 1.5
- w_query: bfloat16 [8192, 4096], P('dp', 'mp'), may hold values from -2 to 2
- key_projection_weight: bfloat16 [8192, 512], P('dp', 'mp'), may hold values from -2 to 2
- value_projection_weight: bfloat16 [8192, 512], P('dp', 'mp'), may hold values from -0.0625 to 0.0625
- w_out: bfloat16 [4096, 8192], P('mp', 'dp'), may hold values from -0.09375 to 0.09375
- final_gain: bfloat16 [8192], P('mp'), may hold values from 0.5 to 1.5
- unembed: bfloat16 [64128, 8192], P('dp', 'mp'), may hold values from -0.29882812 to 0.29882812
- clean_ids: int32 [64], replicated, may hold values from 0 to 64127, as said below
- corrupt_ids: int32 [64], replicated, may hold values from 0 to 64127
Outputs:
- head_out: bfloat16 [16384, 4096], P('dp', 'mp')
- scores: float32 [64, 32], P('dp', 'mp')
- metric: float32 [64], P('dp')
Inputs may be any that keep to these rules, and one draw needn't show every extreme that they name: `clean_ids`: split the ids into 64 aligned blocks of equal size and number the groups of 1 sequence alike; the block of a clean answer, minus the number of its sequence's group, taken modulo the number of blocks, is drawn so that every such offset occurs for some sequence.
All inputs are finite; a program needn't handle non-finite values.
Results may differ from a plain program's by a relative error of at most 0.015.
Values may be sent and summed in bfloat16 or wider, within the bound.
No kernel may reach another device: no remote copies, remote signals or barrier semaphores. Data moves between devices by JAX's collectives and lax.ppermute only.
A program may use at most 128 MiB of HBM per device.

v0:
```python
import math
import jax
import jax.numpy as jnp
from jax import lax
from jax.sharding import Mesh, PartitionSpec as P

MODEL_WIDTH = 8192
HEAD_SIZE = 128
LENGTH = 256
TOKENS = 16384
DP = ("zl", "y", "x")
MP = ("zh", "c")
F32 = jnp.float32
BF16 = jnp.bfloat16


def from_everyone(value, axis):
    count = lax.axis_size(axis)
    return lax.all_to_all(
        jnp.broadcast_to(value[None], (count, *value.shape)), axis, 0, 0, tiled=True
    )


def send(value, route):
    pairs = []
    for x in range(4):
        for c in range(2):
            to = route(x, c)
            if to is not None:
                pairs.append((x * 2 + c, to[0] % 4 * 2 + to[1]))
    return lax.ppermute(value, ("x", "c"), pairs)


def rotary_tables():
    half = HEAD_SIZE // 2
    positions = jnp.arange(LENGTH, dtype=F32)
    inv_freq = jnp.exp(jnp.arange(half, dtype=F32) * (-2.0 * math.log(500000.0) / HEAD_SIZE))
    angles = positions[:, None] * inv_freq[None, :]
    return (jnp.cos(angles)[:, None, :], jnp.sin(angles)[:, None, :])


def rotate(t, cos, sin):
    half = HEAD_SIZE // 2
    lo, hi = (t[..., :half], t[..., half:])
    return jnp.concatenate([lo * cos - hi * sin, hi * cos + lo * sin], axis=-1)


def ring_share(block, core):
    pa = send(block, lambda x, c: (x - 1, 0) if c == 0 else (x + 1, 1))
    pb = send(block, lambda x, c: (x + 1, 1) if c == 0 else (x - 1, 0))
    pc = send(block, lambda x, c: (x + 2, 1) if c == 0 else (x, 0))
    pd = send(block, lambda x, c: None if c == 0 else (x + 2, 1))
    first = core == 0
    f0 = jnp.concatenate([jnp.where(first, block, pc), jnp.where(first, pa, pb)], axis=0)
    f1 = jnp.concatenate([jnp.where(first, pc, pd), jnp.where(first, pb, pa)], axis=0)
    return (f0, f1)


def per_device(tokens, gain, w_query, w_key, w_value, w_out, final_gain, unembed, clean, corrupt):
    zh, core, x = (lax.axis_index("zh"), lax.axis_index("c"), lax.axis_index("x"))
    odd = x % 2
    with jax.named_scope("weights"):
        wkv = jnp.concatenate([w_key, w_value], axis=1)
        width = w_query.shape[1] // 2
        mine = lax.dynamic_slice_in_dim(w_query, odd * width, width, 1)
        other = lax.dynamic_slice_in_dim(w_query, (1 - odd) * width, width, 1)
        pa = send(jnp.concatenate([mine, wkv], axis=1), lambda x, c: (2 * c + x % 2, x // 2))
        pb = send(jnp.concatenate([other, wkv], axis=1), lambda x, c: (2 * c + 1 - x % 2, x // 2))
        rows = jnp.concatenate([jnp.where(odd == 0, pa, pb), jnp.where(odd == 0, pb, pa)], axis=0)
        along_z = lax.all_gather(rows, "zl", axis=0)
        order = [2 * zh, 2 * zh + 1, 2 - 2 * zh, 3 - 2 * zh]
        weights = [
            lax.all_gather(
                lax.dynamic_index_in_dim(along_z, m, 0, keepdims=False),
                ("y", "c"),
                axis=0,
                tiled=True,
            )
            for m in order
        ]
    with jax.named_scope("tokens"):
        far = lax.ppermute(tokens, "zh", [(0, 1), (1, 0)])
        chunks = ring_share(tokens, core) + ring_share(far, core)
    with jax.named_scope("direction"):
        vocab_rows = unembed.shape[0]
        dp_index = lax.axis_index(DP)
        ids = dp_index * vocab_rows + jnp.arange(vocab_rows, dtype=jnp.int32)
        one_hot = (clean[:, None] == ids[None, :]).astype(F32) - (
            corrupt[:, None] == ids[None, :]
        ).astype(F32)
        found = jnp.dot(one_hot.astype(BF16), unembed, preferred_element_type=F32)
        direction = jnp.sum(lax.all_to_all(found[:, None], DP, 0, 0, tiled=True), axis=0)
        weighted = final_gain.astype(F32) * direction[0]
        both = jnp.stack([weighted, tokens[LENGTH - 1].astype(F32)])
        wide = jnp.moveaxis(from_everyone(both, MP), 0, 1).reshape(2, 64, 128)
        columns = lax.all_to_all(jnp.moveaxis(wide, 1, 0), DP, 0, 0, tiled=True)
        weighted_cols, token_cols = (columns[:, 0], columns[:, 1])
        back_w = lax.dot_general(
            weighted_cols.astype(BF16), w_out, (((1,), (1,)), ((), ())), preferred_element_type=F32
        )
        grad_w = jnp.sum(lax.all_to_all(back_w[:, None], DP, 0, 0, tiled=True), axis=0)[0]
    with jax.named_scope("project"):
        acc, squares = (0.0, 0.0)
        for m, chunk, weight in zip(order, chunks, weights):
            t = chunk.astype(F32)
            g = lax.dynamic_slice_in_dim(gain, m * t.shape[1], t.shape[1], 0).astype(F32)
            squares = squares + jnp.sum(t * t, axis=1, keepdims=True)
            acc = acc + jnp.dot((t * g).astype(BF16), weight, preferred_element_type=F32)
        acc = acc * lax.rsqrt(squares / MODEL_WIDTH + 1e-05)
        heads = width // HEAD_SIZE
        acc = acc.reshape(2, LENGTH, heads + 2, HEAD_SIZE)
        cos, sin = rotary_tables()
        queries = rotate(acc[:, :, :heads], cos, sin).astype(BF16)
        keys = rotate(acc[:, :, heads : heads + 1], cos, sin)[:, :, 0].astype(BF16)
        values = acc[:, :, heads + 1].astype(BF16)
    with jax.named_scope("attend"):
        logits = jnp.einsum("btgd,bsd->bgts", queries, keys, preferred_element_type=F32)
        logits = logits / math.sqrt(HEAD_SIZE)
        causal = jnp.arange(LENGTH)[:, None] >= jnp.arange(LENGTH)[None, :]
        logits = jnp.where(causal, logits, -1e30)
        top = jnp.max(logits, axis=-1, keepdims=True)
        e = jnp.exp(logits - top)
        probs = (e / jnp.sum(e, axis=-1, keepdims=True)).astype(BF16)
        mixed = jnp.einsum("bgts,bsd->btgd", probs, values, preferred_element_type=F32)
        mixed = mixed.astype(BF16).reshape(2, LENGTH, width)
    with jax.named_scope("return_heads"):
        oa = send(mixed[0], lambda x, c: (x, x // 2) if c == 0 else (x + 2, x // 2))
        ob = send(mixed[1], lambda x, c: (x + 1, x // 2) if c == 0 else (x - 1, x // 2))
        head_out = jnp.concatenate(
            [jnp.where(odd == 0, oa, ob), jnp.where(odd == 0, ob, oa)], axis=1
        )
    with jax.named_scope("tail"):
        last = head_out[LENGTH - 1].astype(F32)
        total = jnp.sum(head_out.astype(F32), axis=0)
        every = from_everyone(jnp.stack([last, total]), DP)
        head_mean = jnp.sum(every[:, 1], axis=0) / TOKENS
        part = jnp.dot(every[:, 0].astype(BF16), w_out, preferred_element_type=F32)
        attn_last = jnp.sum(from_everyone(part, MP), axis=0).astype(BF16)
        residual = token_cols + attn_last.astype(F32)
        back_r = lax.dot_general(
            residual.astype(BF16), w_out, (((1,), (1,)), ((), ())), preferred_element_type=F32
        )
        sums = jnp.concatenate(
            [
                jnp.broadcast_to(jnp.sum(residual * residual, axis=1)[:, None], (64, 64)),
                jnp.broadcast_to(jnp.sum(residual * weighted_cols, axis=1)[:, None], (64, 64)),
            ],
            axis=1,
        )
        packed = jnp.concatenate([back_r, sums], axis=1)
        mine = jnp.sum(lax.all_to_all(packed[:, None], DP, 0, 0, tiled=True), axis=0)[0]
        grad_r, square, product = (mine[:1024], mine[1024], mine[1024 + 64])
        inverse = lax.rsqrt(square / MODEL_WIDTH + 1e-05)
        metric = inverse * product
        head_grads = grad_w * inverse - grad_r * (metric * inverse * inverse / MODEL_WIDTH)
        scores = jnp.sum(((head_mean - last) * head_grads).reshape(1, 8, HEAD_SIZE), axis=2)
    return (head_out, scores, metric[None])


def solution(mesh):
    fine = Mesh(mesh.devices.reshape(4, 4, 4, 2, 2), (*DP, *MP))
    in_specs = (
        P(DP, MP),
        P(),
        P(DP, MP),
        P(DP, MP),
        P(DP, MP),
        P(MP, DP),
        P(MP),
        P(DP, MP),
        P(),
        P(),
    )
    out_specs = (P(DP, MP), P(DP, MP), P(DP))
    return jax.shard_map(
        per_device, mesh=fine, in_specs=in_specs, out_specs=out_specs, check_vma=False
    )
```

profile of v0, /device:TPU:2, one launch (start us, length us, event | category | flops | bytes accessed | tf_op | source)
XLA Modules:
  0.0 342.4 jit_solution(12943895693049163494)
XLA Ops:
  9.7 2.4 collective-permute-start.4
  12.1 5.0 %collective-permute-done.4 = bf16[128,768]{1,0:T(8,128)(2,1)S(1)} collective-permute-done((bf16[128,768]{1,0:T(8,128)(2,1)S(1)}, bf16[128,768]{1,0:T(8,128)(2,1)S(1)}, u32[]{:S(2)}, u32[]{:S(2)}) %collective-permute-start.4) | collective-permute-done | bytes 196640 | tf_op jit(solution)/shard_map/weights/ppermute | solution.py:31
  18.0 47.1 %all-gather.11.cloned.1.call-done = bf16[1024,768]{1,0:T(8,128)(2,1)} async-done(((bf16[256,768]{1,0:T(8,128)(2,1)}), bf16[1024,768]{1,0:T(8,128)(2,1)}) %all-gather.11.cloned.1.call-update) | async-done | bytes 1572880 | tf_op jit(solution)/shard_map/weights/all_gather | solution.py:70
  65.1 2.5 constant_dynamic-slice_fusion
  69.0 3.9 %collective-permute-start.6 = (bf16[256,2048]{1,0:T(8,128)(2,1)S(1)}, bf16[256,2048]{1,0:T(8,128)(2,1)}, u32[]{:S(2)}, u32[]{:S(2)}) collective-permute-start(bf16[256,2048]{1,0:T(8,128)(2,1)S(1)} %copy-done.8), channel_id=1, source_target_pairs={{0,2},{2,0},{1,3},{3,1},{4,6},{6,4},{5,7},{7,5},{8,10},{10,8},{9,1... | collective-permute-start | bytes 3145736 | tf_op jit(solution)/shard_map/tokens/ppermute | solution.py:82
  76.1 3.1 convolution_bitcast_fusion
  80.5 9.1 %all-to-all-start.1 = ((f32[64,1,2048]{2,1,0:T(1,128)}), f32[64,1,2048]{2,1,0:T(1,128)S(1)}, u32[]{:S(2)}, u32[]{:S(2)}) async-start(f32[64,1,2048]{2,1,0:T(1,128)} %copy.55), calls=%async_computation.1 | async-start | bytes 1048576 | tf_op jit(solution)/shard_map/direction/all_to_all | solution.py:92
  90.1 2.3 collective-permute-start.2
  94.9 39.4 %all-to-all-done.1 = f32[64,1,2048]{2,1,0:T(1,128)S(1)} async-done(((f32[64,1,2048]{2,1,0:T(1,128)}), f32[64,1,2048]{2,1,0:T(1,128)S(1)}, u32[]{:S(2)}, u32[]{:S(2)}) %all-to-all-start.1) | async-done | bytes 524320 | tf_op jit(solution)/shard_map/direction/all_to_all | solution.py:92
  136.8 3.0 collective-permute-start.9
  145.3 35.7 %collective-permute-done.8 = bf16[256,2048]{1,0:T(8,128)(2,1)S(1)} collective-permute-done((bf16[256,2048]{1,0:T(8,128)(2,1)}, bf16[256,2048]{1,0:T(8,128)(2,1)S(1)}, u32[]{:S(2)}, u32[]{:S(2)}) %collective-permute-start.8) | collective-permute-done | bytes 1048608 | tf_op jit(solution)/shard_map/tokens/ppermute | solution.py:31
  181.0 3.1 collective-permute-done.9
  188.0 5.6 %fusion.11 = f32[512,768]{1,0:T(8,128)} fusion(bf16[1,2048,768]{2,1,0:T(8,128)(2,1)} %all-gather.17.cloned.1.call-done, f32[2048]{0:T(1024)} %get-tuple-element.42, bf16[256,2048]{1,0:T(8,128)(2,1)} %copy-done.1, bf16[256,2048]{1,0:T(8,128)(2,1)} %copy-done.6), kind=kOutput, calls=%fused_computation.19 | convolution fusion | flops 1616904192 | bytes 6823936 | tf_op jit(solution)/shard_map/project/dot_general | solution.py:108
  193.6 5.2 %fusion.13 = f32[512,768]{1,0:T(8,128)} fusion(bf16[1,2048,768]{2,1,0:T(8,128)(2,1)} %all-gather.15.cloned.1.call-done, f32[2048]{0:T(1024)} %get-tuple-element.40, bf16[256,2048]{1,0:T(8,128)(2,1)S(1)} %get-tuple-element.11, bf16[256,2048]{1,0:T(8,128)(2,1)} %copy-done.3), kind=kOutput, calls=%fused_computation.21 | convolution fusion | flops 1616904192 | bytes 6823936 | tf_op jit(solution)/shard_map/project/dot_general | solution.py:108
  198.8 5.3 %fusion.15 = f32[512,768]{1,0:T(8,128)} fusion(bf16[1,2048,768]{2,1,0:T(8,128)(2,1)} %all-gather.13.cloned.1.call-done, f32[2048]{0:T(1024)} %get-tuple-element.41, bf16[256,2048]{1,0:T(8,128)(2,1)S(1)} %get-tuple-element.12, bf16[256,2048]{1,0:T(8,128)(2,1)} %copy-done.2), kind=kOutput, calls=%fused_computation.23 | convolution fusion | flops 1616904192 | bytes 6823936 | tf_op jit(solution)/shard_map/project/dot_general | solution.py:108
  204.1 6.3 %add_multiply_fusion = f32[512,768]{1,0:T(8,128)} fusion(f32[512,768]{1,0:T(8,128)} %fusion.11, f32[512,768]{1,0:T(8,128)} %fusion.15, f32[512,768]{1,0:T(8,128)} %fusion.13, bf16[1,2048,768]{2,1,0:T(8,128)(2,1)} %all-gather.19.cloned.1.call-done, f32[2048]{0:T(1024)} %get-tuple-element.39, bf16[256,2048]{1,0:T(8,128)(2,1)S(1)} %get-tuple-element.9, ...), kind=kOutput, calls=%fused_computation.38 | convolution fusion | flops 1618477056 | bytes 11544576 | tf_op jit(solution)/shard_map/project/dot_general | solution.py:108
  220.4 3.5 %fusion.75 = (f32[2,4,256]{2,1,0:T(4,128)S(1)}, f32[2,4,256,256]{2,3,1,0:T(8,128)}) fusion(pred[256,256]{0,1:T(8,128)(4,1)} %iota_compare_fusion, bf16[2,256,4,64]{3,1,2,0:T(8,128)(2,1)} %get-tuple-element.8, bf16[2,256,4,64]{3,1,2,0:T(8,128)(2,1)S(1)} %get-tuple-element.7, bf16[2,256,1,64]{3,1,0,2:T(8,128)(2,1)S(1)} %copy-done.10, ...), kind=kOutput, calls=%fused_computation.132 | convolution fusion | flops 137625856 | bytes 2826240 | tf_op jit(solution)/shard_map/attend/sub | solution.py:122
  223.9 1.9 fusion.30
  226.8 2.7 collective-permute-start.12
  230.2 3.3 all-to-all-start.2
  233.5 2.7 collective-permute-done.12
  237.2 4.9 %all-to-all-done.2 = f32[4,2,2048]{2,1,0:T(2,128)S(1)} async-done(((f32[4,2,2048]{2,1,0:T(2,128)}), f32[4,2,2048]{2,1,0:T(2,128)S(1)}, u32[]{:S(2)}, u32[]{:S(2)}) %all-to-all-start.2) | async-done | bytes 65568 | tf_op jit(solution)/shard_map/direction/all_to_all | solution.py:19
  243.1 8.4 %all-to-all-start = ((f32[64,2,1024]{2,1,0:T(2,128)}), f32[64,2,1024]{2,1,0:T(2,128)S(1)}, u32[]{:S(2)}, u32[]{:S(2)}) async-start(f32[64,2,1024]{2,1,0:T(2,128)} %broadcast_in_dim.26), calls=%async_computation | async-start | bytes 1048576 | tf_op jit(solution)/shard_map/tail/all_to_all | solution.py:19
  252.3 16.1 %all-to-all-done = f32[64,2,1024]{2,1,0:T(2,128)S(1)} async-done(((f32[64,2,1024]{2,1,0:T(2,128)}), f32[64,2,1024]{2,1,0:T(2,128)S(1)}, u32[]{:S(2)}, u32[]{:S(2)}) %all-to-all-start) | async-done | bytes 524320 | tf_op jit(solution)/shard_map/tail/all_to_all | solution.py:19
  268.3 5.9 %all-to-all-start.3 = ((f32[64,2,128]{2,1,0:T(2,128)}), f32[64,2,128]{2,1,0:T(2,128)S(1)}, u32[]{:S(2)}, u32[]{:S(2)}) async-start(f32[64,2,128]{2,1,0:T(2,128)} %copy.57), calls=%async_computation.3 | async-start | bytes 131072 | tf_op jit(solution)/shard_map/direction/all_to_all | solution.py:96
  274.6 8.9 %all-to-all-done.3 = f32[64,2,128]{2,1,0:T(2,128)S(1)} async-done(((f32[64,2,128]{2,1,0:T(2,128)}), f32[64,2,128]{2,1,0:T(2,128)S(1)}, u32[]{:S(2)}, u32[]{:S(2)}) %all-to-all-start.3) | async-done | bytes 65568 | tf_op jit(solution)/shard_map/direction/all_to_all | solution.py:96
  284.2 3.3 all-to-all-start.5
  288.8 7.3 %all-to-all-done.5 = f32[4,64,128]{2,1,0:T(8,128)S(1)} async-done(((f32[4,64,128]{2,1,0:T(8,128)}), f32[4,64,128]{2,1,0:T(8,128)S(1)}, u32[]{:S(2)}, u32[]{:S(2)}) %all-to-all-start.5) | async-done | bytes 131104 | tf_op jit(solution)/shard_map/tail/all_to_all | solution.py:19
  296.0 6.4 %all-to-all-start.4 = ((f32[64,1,1024]{2,1,0:T(1,128)}), f32[64,1,1024]{2,1,0:T(1,128)S(1)}, u32[]{:S(2)}, u32[]{:S(2)}) async-start(f32[64,1,1024]{2,1,0:T(1,128)} %copy.59), calls=%async_computation.4 | async-start | bytes 524288 | tf_op jit(solution)/shard_map/direction/all_to_all | solution.py:101
  304.0 10.1 %all-to-all-done.4 = f32[64,1,1024]{2,1,0:T(1,128)S(1)} async-done(((f32[64,1,1024]{2,1,0:T(1,128)}), f32[64,1,1024]{2,1,0:T(1,128)S(1)}, u32[]{:S(2)}, u32[]{:S(2)}) %all-to-all-start.4) | async-done | bytes 262176 | tf_op jit(solution)/shard_map/direction/all_to_all | solution.py:101
  314.1 6.0 %all-to-all-start.6 = ((f32[64,1,1152]{2,1,0:T(1,128)}), f32[64,1,1152]{2,1,0:T(1,128)S(1)}, u32[]{:S(2)}, u32[]{:S(2)}) async-start(f32[64,1,1152]{2,1,0:T(1,128)} %copy.62), calls=%async_computation.6 | async-start | bytes 589824 | tf_op jit(solution)/shard_map/tail/all_to_all | solution.py:151
  320.7 11.3 %all-to-all-done.6 = f32[64,1,1152]{2,1,0:T(1,128)S(1)} async-done(((f32[64,1,1152]{2,1,0:T(1,128)}), f32[64,1,1152]{2,1,0:T(1,128)S(1)}, u32[]{:S(2)}, u32[]{:S(2)}) %all-to-all-start.6) | async-done | bytes 294944 | tf_op jit(solution)/shard_map/tail/all_to_all | solution.py:151
  (125 shorter events, 44.0 us)
Async XLA Ops:
  7.2 267.3 %copy-start = (bf16[1024,128]{1,0:T(8,128)(2,1)S(1)}, bf16[1024,128]{1,0:T(8,128)(2,1)}, u32[]{:S(2)}) copy-start(bf16[1024,128]{1,0:T(8,128)(2,1)} %param.15) | copy-start | bytes 786436
  7.2 57.9 %all-gather.11.cloned.1.call-start = ((), (), s32[]{:S(2)}) async-start(), calls=%async_computation.7 | async-start | bytes 1966080 | tf_op jit(solution)/shard_map/weights/all_gather | solution.py:70
  9.1 3.0 collective-permute-start.3
  9.7 7.3 %collective-permute-start.4 = (bf16[128,768]{1,0:T(8,128)(2,1)S(1)}, bf16[128,768]{1,0:T(8,128)(2,1)S(1)}, u32[]{:S(2)}, u32[]{:S(2)}) collective-permute-start(bf16[128,768]{1,0:T(8,128)(2,1)S(1)} %get-tuple-element.38), channel_id=1, source_target_pairs={{0,4},{1,12},{4,0},{5,8},{8,5},{9,13},{12,1},{13,9},{2,6},{3,14},{... | collective-permute-start | bytes 589832 | tf_op jit(solution)/shard_map/weights/ppermute | solution.py:31
  12.1 56.9 %copy-start.8 = (bf16[256,2048]{1,0:T(8,128)(2,1)S(1)}, bf16[256,2048]{1,0:T(8,128)(2,1)}, u32[]{:S(2)}) copy-start(bf16[256,2048]{1,0:T(8,128)(2,1)} %param.10) | copy-start | bytes 3145732
  17.1 58.9 %copy-start.13 = (s32[64]{0:T(128)S(1)}, s32[64]{0:T(128)}, u32[]{:S(2)}) copy-start(s32[64]{0:T(128)} %param.19) | copy-start | bytes 772
  17.1 58.9 %copy-start.14 = (s32[64]{0:T(128)S(1)}, s32[64]{0:T(128)}, u32[]{:S(2)}) copy-start(s32[64]{0:T(128)} %param.18) | copy-start | bytes 772
  17.9 170.1 %all-gather.17.cloned.1.call-start = ((), (), s32[]{:S(2)}) async-start(), calls=%async_computation.10 | async-start | bytes 3538944 | tf_op jit(solution)/shard_map/weights/all_gather | solution.py:73
  67.6 126.0 %all-gather.15.cloned.1.call-start = ((), (), s32[]{:S(2)}) async-start(), calls=%async_computation.9 | async-start | bytes 3538944 | tf_op jit(solution)/shard_map/weights/all_gather | solution.py:73
  68.4 130.5 %all-gather.13.cloned.1.call-start = ((), (), s32[]{:S(2)}) async-start(), calls=%async_computation.8 | async-start | bytes 3538944 | tf_op jit(solution)/shard_map/weights/all_gather | solution.py:73
  68.9 135.2 %all-gather.19.cloned.1.call-start = ((), (), s32[]{:S(2)}) async-start(), calls=%async_computation.11 | async-start | bytes 3538944 | tf_op jit(solution)/shard_map/weights/all_gather | solution.py:73
  69.0 65.6 %collective-permute-start.6 = (bf16[256,2048]{1,0:T(8,128)(2,1)S(1)}, bf16[256,2048]{1,0:T(8,128)(2,1)}, u32[]{:S(2)}, u32[]{:S(2)}) collective-permute-start(bf16[256,2048]{1,0:T(8,128)(2,1)S(1)} %copy-done.8), channel_id=1, source_target_pairs={{0,2},{2,0},{1,3},{3,1},{4,6},{6,4},{5,7},{7,5},{8,10},{10,8},{9,1... | collective-permute-start | bytes 3145736 | tf_op jit(solution)/shard_map/tokens/ppermute | solution.py:82
  72.9 62.4 %collective-permute-start = (bf16[256,2048]{1,0:T(8,128)(2,1)S(1)}, bf16[256,2048]{1,0:T(8,128)(2,1)}, u32[]{:S(2)}, u32[]{:S(2)}) collective-permute-start(bf16[256,2048]{1,0:T(8,128)(2,1)S(1)} %copy-done.8), channel_id=1, source_target_pairs={{0,9},{1,0},{4,13},{5,4},{8,1},{9,8},{12,5},{13,12},{2,11},{3,2},{... | collective-permute-start | bytes 3145736 | tf_op jit(solution)/shard_map/tokens/ppermute | solution.py:31
  74.4 62.4 %collective-permute-start.5 = (bf16[256,2048]{1,0:T(8,128)(2,1)S(1)}, bf16[256,2048]{1,0:T(8,128)(2,1)}, u32[]{:S(2)}, u32[]{:S(2)}) collective-permute-start(bf16[256,2048]{1,0:T(8,128)(2,1)S(1)} %copy-done.8), channel_id=1, source_target_pairs={{1,9},{5,13},{9,1},{13,5},{3,11},{7,15},{11,3},{15,7},{17,25},{21,... | collective-permute-start | bytes 3145736 | tf_op jit(solution)/shard_map/tokens/ppermute | solution.py:31
  76.1 18.2 %copy-start.11 = (bf16[8192]{0:T(1024)(128)(2,1)S(1)}, bf16[8192]{0:T(1024)(128)(2,1)}, u32[]{:S(2)}) copy-start(bf16[8192]{0:T(1024)(128)(2,1)} %param.11) | copy-start | bytes 49156
  80.5 53.8 %all-to-all-start.1 = ((f32[64,1,2048]{2,1,0:T(1,128)}), f32[64,1,2048]{2,1,0:T(1,128)S(1)}, u32[]{:S(2)}, u32[]{:S(2)}) async-start(f32[64,1,2048]{2,1,0:T(1,128)} %copy.55), calls=%async_computation.1 | async-start | bytes 1048576 | tf_op jit(solution)/shard_map/direction/all_to_all | solution.py:92
  89.6 51.6 %collective-permute-start.1 = (bf16[256,2048]{1,0:T(8,128)(2,1)S(1)}, bf16[256,2048]{1,0:T(8,128)(2,1)S(1)}, u32[]{:S(2)}, u32[]{:S(2)}) collective-permute-start(bf16[256,2048]{1,0:T(8,128)(2,1)S(1)} %copy-done.8), channel_id=1, source_target_pairs={{0,12},{1,5},{4,0},{5,9},{8,4},{9,13},{12,8},{13,1},{2,14},{3,7},{... | collective-permute-start | bytes 3145736 | tf_op jit(solution)/shard_map/tokens/ppermute | solution.py:31
  90.1 52.8 %collective-permute-start.2 = (bf16[256,2048]{1,0:T(8,128)(2,1)S(1)}, bf16[256,2048]{1,0:T(8,128)(2,1)}, u32[]{:S(2)}, u32[]{:S(2)}) collective-permute-start(bf16[256,2048]{1,0:T(8,128)(2,1)S(1)} %copy-done.8), channel_id=1, source_target_pairs={{0,5},{1,12},{4,9},{5,0},{8,13},{9,4},{12,1},{13,8},{2,7},{3,14},{... | collective-permute-start | bytes 3145736 | tf_op jit(solution)/shard_map/tokens/ppermute | solution.py:31
  134.6 49.7 %collective-permute-start.10 = (bf16[256,2048]{1,0:T(8,128)(2,1)}, bf16[256,2048]{1,0:T(8,128)(2,1)S(1)}, u32[]{:S(2)}, u32[]{:S(2)}) collective-permute-start(bf16[256,2048]{1,0:T(8,128)(2,1)} %collective-permute-done.6), channel_id=1, source_target_pairs={{1,9},{5,13},{9,1},{13,5},{3,11},{7,15},{11,3},{15,7},{17,25},{21,... | collective-permute-start | bytes 3145736 | tf_op jit(solution)/shard_map/tokens/ppermute | solution.py:31
  135.3 45.7 %collective-permute-start.8 = (bf16[256,2048]{1,0:T(8,128)(2,1)}, bf16[256,2048]{1,0:T(8,128)(2,1)S(1)}, u32[]{:S(2)}, u32[]{:S(2)}) collective-permute-start(bf16[256,2048]{1,0:T(8,128)(2,1)} %collective-permute-done.6), channel_id=1, source_target_pairs={{0,12},{1,5},{4,0},{5,9},{8,4},{9,13},{12,8},{13,1},{2,14},{3,7},{... | collective-permute-start | bytes 3145736 | tf_op jit(solution)/shard_map/tokens/ppermute | solution.py:31
  136.8 47.3 %collective-permute-start.9 = (bf16[256,2048]{1,0:T(8,128)(2,1)}, bf16[256,2048]{1,0:T(8,128)(2,1)S(1)}, u32[]{:S(2)}, u32[]{:S(2)}) collective-permute-start(bf16[256,2048]{1,0:T(8,128)(2,1)} %collective-permute-done.6), channel_id=1, source_target_pairs={{0,5},{1,12},{4,9},{5,0},{8,13},{9,4},{12,1},{13,8},{2,7},{3,14},{... | collective-permute-start | bytes 3145736 | tf_op jit(solution)/shard_map/tokens/ppermute | solution.py:31
  141.2 43.1 %collective-permute-start.7 = (bf16[256,2048]{1,0:T(8,128)(2,1)}, bf16[256,2048]{1,0:T(8,128)(2,1)S(1)}, u32[]{:S(2)}, u32[]{:S(2)}) collective-permute-start(bf16[256,2048]{1,0:T(8,128)(2,1)} %collective-permute-done.6), channel_id=1, source_target_pairs={{0,9},{1,0},{4,13},{5,4},{8,1},{9,8},{12,5},{13,12},{2,11},{3,2},{... | collective-permute-start | bytes 3145736 | tf_op jit(solution)/shard_map/tokens/ppermute | solution.py:31
  198.8 5.3 %copy-start.5 = (bf16[256,2048]{1,0:T(8,128)(2,1)S(1)}, bf16[256,2048]{1,0:T(8,128)(2,1)}, u32[]{:S(2)}) copy-start(bf16[256,2048]{1,0:T(8,128)(2,1)} %copy-done.4) | copy-start | bytes 3145732
  223.9 5.7 %copy-start.12 = (bf16[2048]{0:T(1024)(128)(2,1)S(1)}, bf16[2048]{0:T(1024)(128)(2,1)}, u32[]{:S(2)}) copy-start(bf16[2048]{0:T(1024)(128)(2,1)} %param.16) | copy-start | bytes 12292
  226.0 7.5 %collective-permute-start.11 = (bf16[256,512]{1,0:T(8,128)(2,1)S(1)}, bf16[256,512]{1,0:T(8,128)(2,1)S(1)}, u32[]{:S(2)}, u32[]{:S(2)}) collective-permute-start(bf16[256,512]{1,0:T(8,128)(2,1)S(1)} %copy.53), channel_id=1, source_target_pairs={{0,0},{1,8},{4,4},{5,12},{8,9},{9,1},{12,13},{13,5},{2,2},{3,10},{... | collective-permute-start | bytes 786440 | tf_op jit(solution)/shard_map/return_heads/ppermute | solution.py:31
  226.8 9.4 %collective-permute-start.12 = (bf16[256,512]{1,0:T(8,128)(2,1)S(1)}, bf16[256,512]{1,0:T(8,128)(2,1)S(1)}, u32[]{:S(2)}, u32[]{:S(2)}) collective-permute-start(bf16[256,512]{1,0:T(8,128)(2,1)S(1)} %copy.54), channel_id=1, source_target_pairs={{0,4},{1,12},{4,8},{5,0},{8,13},{9,5},{12,1},{13,9},{2,6},{3,14},{... | collective-permute-start | bytes 786440 | tf_op jit(solution)/shard_map/return_heads/ppermute | solution.py:31
  230.2 11.9 %all-to-all-start.2 = ((f32[4,2,2048]{2,1,0:T(2,128)}), f32[4,2,2048]{2,1,0:T(2,128)S(1)}, u32[]{:S(2)}, u32[]{:S(2)}) async-start(f32[4,2,2048]{2,1,0:T(2,128)} %broadcast_in_dim.28), calls=%async_computation.2 | async-start | bytes 131072 | tf_op jit(solution)/shard_map/direction/all_to_all | solution.py:19
  243.1 25.3 %all-to-all-start = ((f32[64,2,1024]{2,1,0:T(2,128)}), f32[64,2,1024]{2,1,0:T(2,128)S(1)}, u32[]{:S(2)}, u32[]{:S(2)}) async-start(f32[64,2,1024]{2,1,0:T(2,128)} %broadcast_in_dim.26), calls=%async_computation | async-start | bytes 1048576 | tf_op jit(solution)/shard_map/tail/all_to_all | solution.py:19
  268.3 15.2 %all-to-all-start.3 = ((f32[64,2,128]{2,1,0:T(2,128)}), f32[64,2,128]{2,1,0:T(2,128)S(1)}, u32[]{:S(2)}, u32[]{:S(2)}) async-start(f32[64,2,128]{2,1,0:T(2,128)} %copy.57), calls=%async_computation.3 | async-start | bytes 131072 | tf_op jit(solution)/shard_map/direction/all_to_all | solution.py:96
  284.2 11.8 %all-to-all-start.5 = ((f32[4,64,128]{2,1,0:T(8,128)}), f32[4,64,128]{2,1,0:T(8,128)S(1)}, u32[]{:S(2)}, u32[]{:S(2)}) async-start(f32[4,64,128]{2,1,0:T(8,128)} %broadcast_in_dim.30), calls=%async_computation.5 | async-start | bytes 262144 | tf_op jit(solution)/shard_map/tail/all_to_all | solution.py:19
  296.0 18.1 %all-to-all-start.4 = ((f32[64,1,1024]{2,1,0:T(1,128)}), f32[64,1,1024]{2,1,0:T(1,128)S(1)}, u32[]{:S(2)}, u32[]{:S(2)}) async-start(f32[64,1,1024]{2,1,0:T(1,128)} %copy.59), calls=%async_computation.4 | async-start | bytes 524288 | tf_op jit(solution)/shard_map/direction/all_to_all | solution.py:101
  314.1 17.8 %all-to-all-start.6 = ((f32[64,1,1152]{2,1,0:T(1,128)}), f32[64,1,1152]{2,1,0:T(1,128)S(1)}, u32[]{:S(2)}, u32[]{:S(2)}) async-start(f32[64,1,1152]{2,1,0:T(1,128)} %copy.62), calls=%async_computation.6 | async-start | bytes 589824 | tf_op jit(solution)/shard_map/tail/all_to_all | solution.py:151
  (8 other events, 21.6 us)
Sparse Core Ops, SparseCore 0:
  18.0 46.9 all-gather.10
  67.7 30.0 all-gather.16
  99.7 34.6 all-gather.14
  136.1 30.1 all-gather.12
  168.0 30.3 all-gather.18
where the time goes:
time: 344 us; the launch traced here: 342 us
  waiting for transfers between devices  193 us (56%)
  starting transfers between devices  65.8 us (19%)
  matrix products  31.4 us (9%)
  local copies, waits for them, and re-layouts  18.8 us (5%)
  other arithmetic  16.8 us (5%)
  between operations  16.8 us (5%)
    all_gather x1, waiting for transfers between devices, per_device(): along_z = lax.all_gather(rows, 'zl', axis=0)  47.1 us
    ppermute x12, waiting for transfers between devices, send(): return lax.ppermute(value, ('x', 'c'), pairs)  46.6 us
    all_to_all x1, waiting for transfers between devices, per_device(): lax.all_to_all(found[:, None], DP, 0, 0, tiled=True)  39.4 us
    all_to_all x3, waiting for transfers between devices, from_everyone(): lax.all_to_all(jnp.broadcast_to(value[None], (count, *value.shape)), axis...  28.3 us
    dot_general x4, matrix products, per_device(): jnp.dot((t * g).astype(BF16), weight, preferred_element_type=F32)  22.3 us
    ppermute x12, starting transfers between devices, send(): return lax.ppermute(value, ('x', 'c'), pairs)  19.2 us
    all_to_all x3, starting transfers between devices, from_everyone(): lax.all_to_all(jnp.broadcast_to(value[None], (count, *value.shape)), axis...  15 us
    all_to_all x1, waiting for transfers between devices, per_device(): lax.all_to_all(packed[:, None], DP, 0, 0, tiled=True)  11.3 us
  transfers between devices with their start and end apart: 25, of which 12 were waited for; matrix products, arithmetic and copies ran while one was open for 11% of the time, Pallas kernels for 0%

commit v1 on v0

--- a/solution.py
+++ b/solution.py
@@ -1,3 +1,4 @@
+import functools
 import math
 import jax
 import jax.numpy as jnp
@@ -12,6 +13,21 @@
 MP = ("zh", "c")
 F32 = jnp.float32
 BF16 = jnp.bfloat16
+
+
+def ticks_obtain(incoming_x, net_axis, in_dim):
+    return jnp.concatenate(
+        jax.lax.all_to_all(
+            jnp.stack(tuple((incoming_x for _ in range(jax.lax.axis_size(net_axis))))),
+            axis_name=net_axis,
+            split_axis=0,
+            concat_axis=0,
+        ),
+        in_dim,
+    )
+
+
+unit_advance = functools.partial(ticks_obtain, net_axis=("y", "c"), in_dim=0)
 
 
 def from_everyone(value, axis):
@@ -70,13 +86,7 @@
         along_z = lax.all_gather(rows, "zl", axis=0)
         order = [2 * zh, 2 * zh + 1, 2 - 2 * zh, 3 - 2 * zh]
         weights = [
-            lax.all_gather(
-                lax.dynamic_index_in_dim(along_z, m, 0, keepdims=False),
-                ("y", "c"),
-                axis=0,
-                tiled=True,
-            )
-            for m in order
+            unit_advance(lax.dynamic_index_in_dim(along_z, m, 0, keepdims=False)) for m in order
         ]
     with jax.named_scope("tokens"):
         far = lax.ppermute(tokens, "zh", [(0, 1), (1, 0)])

time: 344 us -> 428 us (1.24)
  blocking collectives: 0 us -> 85.3 us
  waiting for transfers between devices: 193 us -> 170 us
  starting transfers between devices: 65.8 us -> 87 us
  matrix products: 31.4 us -> 26.3 us
    all_to_all x0 -> x2, blocking collectives: none -> 85.3 us  [ticks_obtain(): jax.lax.all_to_all(jnp.stack(tuple((incoming_x for _ in range(jax.lax.axi...]
    all_to_all x1, waiting for transfers between devices: 39.4 us -> 0.01 us  [per_device(): lax.all_to_all(found[:, None], DP, 0, 0, tiled=True)]
    ppermute x1, waiting for transfers between devices: 0.01 us -> 16.8 us  [per_device(): far = lax.ppermute(tokens, 'zh', [(0, 1), (1, 0)])]
    all_gather x1, waiting for transfers between devices: 47.1 us -> 35.9 us  [per_device(): along_z = lax.all_gather(rows, 'zl', axis=0)]
    ppermute x12, waiting for transfers between devices: 46.6 us -> 56.5 us  [send(): return lax.ppermute(value, ('x', 'c'), pairs)]
    all_to_all x3, starting transfers between devices: 15 us -> 24.9 us  [from_everyone(): lax.all_to_all(jnp.broadcast_to(value[None], (count, *value.shape)), axis...]
    all_to_all x0 -> x2, starting transfers between devices: none -> 9.2 us  [ticks_obtain(): jax.lax.all_to_all(jnp.stack(tuple((incoming_x for _ in range(jax.lax.axi...]
    all_to_all x1, starting transfers between devices: 9.1 us -> 14.4 us  [per_device(): lax.all_to_all(found[:, None], DP, 0, 0, tiled=True)]
  transfers between devices with their start and end apart: 25 -> 23, of which waited for: 12 -> 12; matrix products, arithmetic and copies ran while one was open for 11% -> 9% of each run, Pallas kernels for 0% -> 0%
where the time goes in v1:
time: 428 us; the launch traced here: 427 us
  waiting for transfers between devices  170 us (40%)
  starting transfers between devices  87 us (20%)
  blocking collectives  85.3 us (20%)
  matrix products  26.3 us (6%)
  local copies, waits for them, and re-layouts  22.2 us (5%)
  other arithmetic  19.2 us (4%)
  between operations  17.1 us (4%)
    all_to_all x2, blocking collectives, ticks_obtain(): jax.lax.all_to_all(jnp.stack(tuple((incoming_x for _ in range(jax.lax.axi...  85.3 us
    ppermute x12, waiting for transfers between devices, send(): return lax.ppermute(value, ('x', 'c'), pairs)  56.5 us
    all_gather x1, waiting for transfers between devices, per_device(): along_z = lax.all_gather(rows, 'zl', axis=0)  35.9 us
    all_to_all x3, waiting for transfers between devices, from_everyone(): lax.all_to_all(jnp.broadcast_to(value[None], (count, *value.shape)), axis...  30.4 us
    all_to_all x3, starting transfers between devices, from_everyone(): lax.all_to_all(jnp.broadcast_to(value[None], (count, *value.shape)), axis...  24.9 us
    dot_general x4, matrix products, per_device(): jnp.dot((t * g).astype(BF16), weight, preferred_element_type=F32)  17.2 us
    ppermute x1, waiting for transfers between devices, per_device(): far = lax.ppermute(tokens, 'zh', [(0, 1), (1, 0)])  16.8 us
    ppermute x12, starting transfers between devices, send(): return lax.ppermute(value, ('x', 'c'), pairs)  15.6 us
  transfers between devices with their start and end apart: 23, of which 12 were waited for; matrix products, arithmetic and copies ran while one was open for 9% of the time, Pallas kernels for 0%

profile of v1, /device:TPU:2, one launch (start us, length us, event | category | flops | bytes accessed | tf_op | source)
XLA Modules:
  0.0 427.0 jit_solution(17555884296295741904)
XLA Ops:
  9.8 2.4 collective-permute-start.4
  12.1 5.0 %collective-permute-done.4 = bf16[128,768]{1,0:T(8,128)(2,1)S(1)} collective-permute-done((bf16[128,768]{1,0:T(8,128)(2,1)S(1)}, bf16[128,768]{1,0:T(8,128)(2,1)S(1)}, u32[]{:S(2)}, u32[]{:S(2)}) %collective-permute-start.4) | collective-permute-done | bytes 196640 | tf_op jit(solution)/shard_map/weights/ppermute | solution.py:47
  18.0 3.1 convolution_bitcast_fusion
  22.4 14.4 %all-to-all-start.5 = ((f32[64,1,2048]{2,1,0:T(1,128)}), f32[64,1,2048]{2,1,0:T(1,128)S(1)}, u32[]{:S(2)}, u32[]{:S(2)}) async-start(f32[64,1,2048]{2,1,0:T(1,128)} %copy.55), calls=%async_computation.5 | async-start | bytes 1048576 | tf_op jit(solution)/shard_map/direction/all_to_all | solution.py:102
  36.8 35.9 %all-gather.3.cloned.1.call-done = bf16[1024,768]{1,0:T(8,128)(2,1)} async-done(((bf16[256,768]{1,0:T(8,128)(2,1)}), bf16[1024,768]{1,0:T(8,128)(2,1)}) %all-gather.3.cloned.1.call-update) | async-done | bytes 1572880 | tf_op jit(solution)/shard_map/weights/all_gather | solution.py:86
  74.4 43.1 %all_to_all.55 = bf16[8,256,768]{2,1,0:T(8,128)(2,1)} all-to-all(bf16[8,256,768]{2,1,0:T(8,128)(2,1)S(1)} %stack.18), channel_id=1, replica_groups=mesh['zl'=4,'y'=4,'x'=4,'zh'=2,'c'=2] {'y','c'}, dimensions={0} | all-to-all | bytes 6291456 | tf_op jit(solution)/shard_map/weights/all_to_all | solution.py:20
  117.7 42.1 %all_to_all.56 = bf16[8,256,768]{2,1,0:T(8,128)(2,1)} all-to-all(bf16[8,256,768]{2,1,0:T(8,128)(2,1)S(1)} %stack.17), channel_id=1, replica_groups=mesh['zl'=4,'y'=4,'x'=4,'zh'=2,'c'=2] {'y','c'}, dimensions={0} | all-to-all | bytes 6291456 | tf_op jit(solution)/shard_map/weights/all_to_all | solution.py:20
  161.7 4.6 %all-to-all-start = ((bf16[8,256,768]{2,1,0:T(8,128)(2,1)}), bf16[8,256,768]{2,1,0:T(8,128)(2,1)}, u32[]{:S(2)}, u32[]{:S(2)}) async-start(bf16[8,256,768]{2,1,0:T(8,128)(2,1)} %stack.16), calls=%async_computation | async-start | bytes 6291456 | tf_op jit(solution)/shard_map/weights/all_to_all | solution.py:20
  166.3 4.6 %collective-permute-start.6 = (bf16[256,2048]{1,0:T(8,128)(2,1)S(1)}, bf16[256,2048]{1,0:T(8,128)(2,1)}, u32[]{:S(2)}, u32[]{:S(2)}) collective-permute-start(bf16[256,2048]{1,0:T(8,128)(2,1)S(1)} %copy-done.10), channel_id=1, source_target_pairs={{0,2},{2,0},{1,3},{3,1},{4,6},{6,4},{5,7},{7,5},{8,10},{10,8},{9,1... | collective-permute-start | bytes 3145736 | tf_op jit(solution)/shard_map/tokens/ppermute | solution.py:92
  172.6 3.2 collective-permute-start
  179.3 16.8 %collective-permute-done.6 = bf16[256,2048]{1,0:T(8,128)(2,1)} collective-permute-done((bf16[256,2048]{1,0:T(8,128)(2,1)S(1)}, bf16[256,2048]{1,0:T(8,128)(2,1)}, u32[]{:S(2)}, u32[]{:S(2)}) %collective-permute-start.6) | collective-permute-done | bytes 1048608 | tf_op jit(solution)/shard_map/tokens/ppermute | solution.py:92
  197.7 2.1 collective-permute-start.9
  202.3 22.0 %collective-permute-done.2 = bf16[256,2048]{1,0:T(8,128)(2,1)} collective-permute-done((bf16[256,2048]{1,0:T(8,128)(2,1)S(1)}, bf16[256,2048]{1,0:T(8,128)(2,1)}, u32[]{:S(2)}, u32[]{:S(2)}) %collective-permute-start.2) | collective-permute-done | bytes 1048608 | tf_op jit(solution)/shard_map/tokens/ppermute | solution.py:47
  230.3 4.6 %all-to-all-start.3 = ((bf16[8,256,768]{2,1,0:T(8,128)(2,1)}), bf16[8,256,768]{2,1,0:T(8,128)(2,1)}, u32[]{:S(2)}, u32[]{:S(2)}) async-start(bf16[8,256,768]{2,1,0:T(8,128)(2,1)} %stack.19), calls=%async_computation.3 | async-start | bytes 6291456 | tf_op jit(solution)/shard_map/weights/all_to_all | solution.py:20
  234.9 29.3 %collective-permute-done.9 = bf16[256,2048]{1,0:T(8,128)(2,1)} collective-permute-done((bf16[256,2048]{1,0:T(8,128)(2,1)}, bf16[256,2048]{1,0:T(8,128)(2,1)}, u32[]{:S(2)}, u32[]{:S(2)}) %collective-permute-start.9) | collective-permute-done | bytes 1048608 | tf_op jit(solution)/shard_map/tokens/ppermute | solution.py:47
  270.1 3.0 fusion.11
  273.1 3.0 fusion.13
  276.1 5.0 %fusion.15 = f32[512,768]{1,0:T(8,128)} fusion(bf16[2048,768]{1,0:T(8,128)(2,1)} %bitcast.2, f32[2048]{0:T(1024)S(1)} %copy-done.16, bf16[256,2048]{1,0:T(8,128)(2,1)S(1)} %get-tuple-element.12, bf16[256,2048]{1,0:T(8,128)(2,1)S(1)} %copy-done.2), kind=kOutput, calls=%fused_computation.21 | convolution fusion | flops 1616904192 | bytes 6823936 | tf_op jit(solution)/shard_map/project/dot_general | solution.py:118
  281.1 6.3 %add_multiply_fusion = f32[512,768]{1,0:T(8,128)} fusion(f32[512,768]{1,0:T(8,128)} %fusion.11, f32[512,768]{1,0:T(8,128)} %fusion.15, f32[512,768]{1,0:T(8,128)} %fusion.13, bf16[2048,768]{1,0:T(8,128)(2,1)} %bitcast.8, f32[2048]{0:T(1024)} %get-tuple-element.39, bf16[256,2048]{1,0:T(8,128)(2,1)S(1)} %get-tuple-element.9, ...), kind=kOutput, calls=%fused_computation.34 | convolution fusion | flops 1618477056 | bytes 11544576 | tf_op jit(solution)/shard_map/project/dot_general | solution.py:118
  297.4 3.5 fusion.69
  305.2 6.2 %all-to-all-start.6 = ((f32[4,2,2048]{2,1,0:T(2,128)}), f32[4,2,2048]{2,1,0:T(2,128)S(1)}, u32[]{:S(2)}, u32[]{:S(2)}) async-start(f32[4,2,2048]{2,1,0:T(2,128)} %broadcast_in_dim.28), calls=%async_computation.6 | async-start | bytes 131072 | tf_op jit(solution)/shard_map/direction/all_to_all | solution.py:35
  312.4 7.1 %all-to-all-done.6 = f32[4,2,2048]{2,1,0:T(2,128)S(1)} async-done(((f32[4,2,2048]{2,1,0:T(2,128)}), f32[4,2,2048]{2,1,0:T(2,128)S(1)}, u32[]{:S(2)}, u32[]{:S(2)}) %all-to-all-start.6) | async-done | bytes 65568 | tf_op jit(solution)/shard_map/direction/all_to_all | solution.py:35
  320.4 15.3 %all-to-all-start.4 = ((f32[64,2,1024]{2,1,0:T(2,128)}), f32[64,2,1024]{2,1,0:T(2,128)S(1)}, u32[]{:S(2)}, u32[]{:S(2)}) async-start(f32[64,2,1024]{2,1,0:T(2,128)} %broadcast_in_dim.26), calls=%async_computation.4 | async-start | bytes 1048576 | tf_op jit(solution)/shard_map/tail/all_to_all | solution.py:35
  336.5 16.1 %all-to-all-done.4 = f32[64,2,1024]{2,1,0:T(2,128)S(1)} async-done(((f32[64,2,1024]{2,1,0:T(2,128)}), f32[64,2,1024]{2,1,0:T(2,128)S(1)}, u32[]{:S(2)}, u32[]{:S(2)}) %all-to-all-start.4) | async-done | bytes 524320 | tf_op jit(solution)/shard_map/tail/all_to_all | solution.py:35
  352.6 5.9 %all-to-all-start.7 = ((f32[64,2,128]{2,1,0:T(2,128)}), f32[64,2,128]{2,1,0:T(2,128)S(1)}, u32[]{:S(2)}, u32[]{:S(2)}) async-start(f32[64,2,128]{2,1,0:T(2,128)} %copy.57), calls=%async_computation.7 | async-start | bytes 131072 | tf_op jit(solution)/shard_map/direction/all_to_all | solution.py:106
  358.8 8.9 %all-to-all-done.7 = f32[64,2,128]{2,1,0:T(2,128)S(1)} async-done(((f32[64,2,128]{2,1,0:T(2,128)}), f32[64,2,128]{2,1,0:T(2,128)S(1)}, u32[]{:S(2)}, u32[]{:S(2)}) %all-to-all-start.7) | async-done | bytes 65568 | tf_op jit(solution)/shard_map/direction/all_to_all | solution.py:106
  368.4 3.3 all-to-all-start.9
  373.0 7.3 %all-to-all-done.9 = f32[4,64,128]{2,1,0:T(8,128)S(1)} async-done(((f32[4,64,128]{2,1,0:T(8,128)}), f32[4,64,128]{2,1,0:T(8,128)S(1)}, u32[]{:S(2)}, u32[]{:S(2)}) %all-to-all-start.9) | async-done | bytes 131104 | tf_op jit(solution)/shard_map/tail/all_to_all | solution.py:35
  380.3 6.4 %all-to-all-start.8 = ((f32[64,1,1024]{2,1,0:T(1,128)}), f32[64,1,1024]{2,1,0:T(1,128)S(1)}, u32[]{:S(2)}, u32[]{:S(2)}) async-start(f32[64,1,1024]{2,1,0:T(1,128)} %copy.59), calls=%async_computation.8 | async-start | bytes 524288 | tf_op jit(solution)/shard_map/direction/all_to_all | solution.py:111
  388.2 10.1 %all-to-all-done.8 = f32[64,1,1024]{2,1,0:T(1,128)S(1)} async-done(((f32[64,1,1024]{2,1,0:T(1,128)}), f32[64,1,1024]{2,1,0:T(1,128)S(1)}, u32[]{:S(2)}, u32[]{:S(2)}) %all-to-all-start.8) | async-done | bytes 262176 | tf_op jit(solution)/shard_map/direction/all_to_all | solution.py:111
  398.4 6.0 %all-to-all-start.10 = ((f32[64,1,1152]{2,1,0:T(1,128)}), f32[64,1,1152]{2,1,0:T(1,128)S(1)}, u32[]{:S(2)}, u32[]{:S(2)}) async-start(f32[64,1,1152]{2,1,0:T(1,128)} %copy.62), calls=%async_computation.10 | async-start | bytes 589824 | tf_op jit(solution)/shard_map/tail/all_to_all | solution.py:161
  404.9 11.3 %all-to-all-done.10 = f32[64,1,1152]{2,1,0:T(1,128)S(1)} async-done(((f32[64,1,1152]{2,1,0:T(1,128)}), f32[64,1,1152]{2,1,0:T(1,128)S(1)}, u32[]{:S(2)}, u32[]{:S(2)}) %all-to-all-start.10) | async-done | bytes 294944 | tf_op jit(solution)/shard_map/tail/all_to_all | solution.py:161
  (137 shorter events, 52.0 us)
Async XLA Ops:
  7.2 351.5 %copy-start = (bf16[1024,128]{1,0:T(8,128)(2,1)S(1)}, bf16[1024,128]{1,0:T(8,128)(2,1)}, u32[]{:S(2)}) copy-start(bf16[1024,128]{1,0:T(8,128)(2,1)} %param.15) | copy-start | bytes 786436
  7.2 10.8 %copy-start.20 = (s32[64]{0:T(128)S(1)}, s32[64]{0:T(128)}, u32[]{:S(2)}) copy-start(s32[64]{0:T(128)} %param.19) | copy-start | bytes 772
  7.2 10.8 %copy-start.21 = (s32[64]{0:T(128)S(1)}, s32[64]{0:T(128)}, u32[]{:S(2)}) copy-start(s32[64]{0:T(128)} %param.18) | copy-start | bytes 772
  7.2 65.5 %all-gather.3.cloned.1.call-start = ((), (), s32[]{:S(2)}) async-start(), calls=%async_computation.11 | async-start | bytes 1966080 | tf_op jit(solution)/shard_map/weights/all_gather | solution.py:86
  9.1 3.0 collective-permute-start.3
  9.8 7.3 %collective-permute-start.4 = (bf16[128,768]{1,0:T(8,128)(2,1)S(1)}, bf16[128,768]{1,0:T(8,128)(2,1)S(1)}, u32[]{:S(2)}, u32[]{:S(2)}) collective-permute-start(bf16[128,768]{1,0:T(8,128)(2,1)S(1)} %get-tuple-element.38), channel_id=1, source_target_pairs={{0,4},{1,12},{4,0},{5,8},{8,5},{9,13},{12,1},{13,9},{2,6},{3,14},{... | collective-permute-start | bytes 589832 | tf_op jit(solution)/shard_map/weights/ppermute | solution.py:47
  22.4 51.8 %all-to-all-start.5 = ((f32[64,1,2048]{2,1,0:T(1,128)}), f32[64,1,2048]{2,1,0:T(1,128)S(1)}, u32[]{:S(2)}, u32[]{:S(2)}) async-start(f32[64,1,2048]{2,1,0:T(1,128)} %copy.55), calls=%async_computation.5 | async-start | bytes 1048576 | tf_op jit(solution)/shard_map/direction/all_to_all | solution.py:102
  161.7 4.6 %copy-start.10 = (bf16[256,2048]{1,0:T(8,128)(2,1)S(1)}, bf16[256,2048]{1,0:T(8,128)(2,1)}, u32[]{:S(2)}) copy-start(bf16[256,2048]{1,0:T(8,128)(2,1)} %param.10) | copy-start | bytes 3145732
  161.7 16.6 %copy-start.13 = (bf16[8192]{0:T(1024)(128)(2,1)S(1)}, bf16[8192]{0:T(1024)(128)(2,1)}, u32[]{:S(2)}) copy-start(bf16[8192]{0:T(1024)(128)(2,1)} %param.11) | copy-start | bytes 49156
  161.7 66.7 %all-to-all-start = ((bf16[8,256,768]{2,1,0:T(8,128)(2,1)}), bf16[8,256,768]{2,1,0:T(8,128)(2,1)}, u32[]{:S(2)}, u32[]{:S(2)}) async-start(bf16[8,256,768]{2,1,0:T(8,128)(2,1)} %stack.16), calls=%async_computation | async-start | bytes 6291456 | tf_op jit(solution)/shard_map/weights/all_to_all | solution.py:20
  166.3 29.7 %collective-permute-start.6 = (bf16[256,2048]{1,0:T(8,128)(2,1)S(1)}, bf16[256,2048]{1,0:T(8,128)(2,1)}, u32[]{:S(2)}, u32[]{:S(2)}) collective-permute-start(bf16[256,2048]{1,0:T(8,128)(2,1)S(1)} %copy-done.10), channel_id=1, source_target_pairs={{0,2},{2,0},{1,3},{3,1},{4,6},{6,4},{5,7},{7,5},{8,10},{10,8},{9,1... | collective-permute-start | bytes 3145736 | tf_op jit(solution)/shard_map/tokens/ppermute | solution.py:92
  171.0 26.7 %collective-permute-start.5 = (bf16[256,2048]{1,0:T(8,128)(2,1)S(1)}, bf16[256,2048]{1,0:T(8,128)(2,1)}, u32[]{:S(2)}, u32[]{:S(2)}) collective-permute-start(bf16[256,2048]{1,0:T(8,128)(2,1)S(1)} %copy-done.10), channel_id=1, source_target_pairs={{1,9},{5,13},{9,1},{13,5},{3,11},{7,15},{11,3},{15,7},{17,25},{21,... | collective-permute-start | bytes 3145736 | tf_op jit(solution)/shard_map/tokens/ppermute | solution.py:47
  172.6 27.2 %collective-permute-start = (bf16[256,2048]{1,0:T(8,128)(2,1)S(1)}, bf16[256,2048]{1,0:T(8,128)(2,1)}, u32[]{:S(2)}, u32[]{:S(2)}) collective-permute-start(bf16[256,2048]{1,0:T(8,128)(2,1)S(1)} %copy-done.10), channel_id=1, source_target_pairs={{0,9},{1,0},{4,13},{5,4},{8,1},{9,8},{12,5},{13,12},{2,11},{3,2},{... | collective-permute-start | bytes 3145736 | tf_op jit(solution)/shard_map/tokens/ppermute | solution.py:47
  175.8 48.6 %collective-permute-start.2 = (bf16[256,2048]{1,0:T(8,128)(2,1)S(1)}, bf16[256,2048]{1,0:T(8,128)(2,1)}, u32[]{:S(2)}, u32[]{:S(2)}) collective-permute-start(bf16[256,2048]{1,0:T(8,128)(2,1)S(1)} %copy-done.10), channel_id=1, source_target_pairs={{0,5},{1,12},{4,9},{5,0},{8,13},{9,4},{12,1},{13,8},{2,7},{3,14},{... | collective-permute-start | bytes 3145736 | tf_op jit(solution)/shard_map/tokens/ppermute | solution.py:47
  175.8 49.3 %collective-permute-start.1 = (bf16[256,2048]{1,0:T(8,128)(2,1)S(1)}, bf16[256,2048]{1,0:T(8,128)(2,1)}, u32[]{:S(2)}, u32[]{:S(2)}) collective-permute-start(bf16[256,2048]{1,0:T(8,128)(2,1)S(1)} %copy-done.10), channel_id=1, source_target_pairs={{0,12},{1,5},{4,0},{5,9},{8,4},{9,13},{12,8},{13,1},{2,14},{3,7},{... | collective-permute-start | bytes 3145736 | tf_op jit(solution)/shard_map/tokens/ppermute | solution.py:47
  196.1 70.0 %collective-permute-start.10 = (bf16[256,2048]{1,0:T(8,128)(2,1)}, bf16[256,2048]{1,0:T(8,128)(2,1)}, u32[]{:S(2)}, u32[]{:S(2)}) collective-permute-start(bf16[256,2048]{1,0:T(8,128)(2,1)} %collective-permute-done.6), channel_id=1, source_target_pairs={{1,9},{5,13},{9,1},{13,5},{3,11},{7,15},{11,3},{15,7},{17,25},{21,... | collective-permute-start | bytes 3145736 | tf_op jit(solution)/shard_map/tokens/ppermute | solution.py:47
  197.7 66.5 %collective-permute-start.9 = (bf16[256,2048]{1,0:T(8,128)(2,1)}, bf16[256,2048]{1,0:T(8,128)(2,1)}, u32[]{:S(2)}, u32[]{:S(2)}) collective-permute-start(bf16[256,2048]{1,0:T(8,128)(2,1)} %collective-permute-done.6), channel_id=1, source_target_pairs={{0,5},{1,12},{4,9},{5,0},{8,13},{9,4},{12,1},{13,8},{2,7},{3,14},{... | collective-permute-start | bytes 3145736 | tf_op jit(solution)/shard_map/tokens/ppermute | solution.py:47
  199.8 64.5 %collective-permute-start.8 = (bf16[256,2048]{1,0:T(8,128)(2,1)}, bf16[256,2048]{1,0:T(8,128)(2,1)}, u32[]{:S(2)}, u32[]{:S(2)}) collective-permute-start(bf16[256,2048]{1,0:T(8,128)(2,1)} %collective-permute-done.6), channel_id=1, source_target_pairs={{0,12},{1,5},{4,0},{5,9},{8,4},{9,13},{12,8},{13,1},{2,14},{3,7},{... | collective-permute-start | bytes 3145736 | tf_op jit(solution)/shard_map/tokens/ppermute | solution.py:47
  202.3 24.5 %copy-start.1 = (bf16[256,2048]{1,0:T(8,128)(2,1)}, bf16[256,2048]{1,0:T(8,128)(2,1)S(1)}, u32[]{:S(2)}) copy-start(bf16[256,2048]{1,0:T(8,128)(2,1)S(1)} %get-tuple-element.24) | copy-start | bytes 3145732
  202.3 24.5 %copy-start.3 = (bf16[256,2048]{1,0:T(8,128)(2,1)}, bf16[256,2048]{1,0:T(8,128)(2,1)S(1)}, u32[]{:S(2)}) copy-start(bf16[256,2048]{1,0:T(8,128)(2,1)S(1)} %get-tuple-element.23) | copy-start | bytes 3145732
  224.4 41.7 %collective-permute-start.7 = (bf16[256,2048]{1,0:T(8,128)(2,1)}, bf16[256,2048]{1,0:T(8,128)(2,1)}, u32[]{:S(2)}, u32[]{:S(2)}) collective-permute-start(bf16[256,2048]{1,0:T(8,128)(2,1)} %collective-permute-done.6), channel_id=1, source_target_pairs={{0,9},{1,0},{4,13},{5,4},{8,1},{9,8},{12,5},{13,12},{2,11},{3,2},{... | collective-permute-start | bytes 3145736 | tf_op jit(solution)/shard_map/tokens/ppermute | solution.py:47
  230.3 50.8 %all-to-all-start.3 = ((bf16[8,256,768]{2,1,0:T(8,128)(2,1)}), bf16[8,256,768]{2,1,0:T(8,128)(2,1)}, u32[]{:S(2)}, u32[]{:S(2)}) async-start(bf16[8,256,768]{2,1,0:T(8,128)(2,1)} %stack.19), calls=%async_computation.3 | async-start | bytes 6291456 | tf_op jit(solution)/shard_map/weights/all_to_all | solution.py:20
  276.1 5.0 %copy-start.6 = (bf16[256,2048]{1,0:T(8,128)(2,1)S(1)}, bf16[256,2048]{1,0:T(8,128)(2,1)}, u32[]{:S(2)}) copy-start(bf16[256,2048]{1,0:T(8,128)(2,1)} %copy-done.5) | copy-start | bytes 3145732
  300.9 3.7 copy-start.19
  303.1 8.3 %collective-permute-start.12 = (bf16[256,512]{1,0:T(8,128)(2,1)S(1)}, bf16[256,512]{1,0:T(8,128)(2,1)S(1)}, u32[]{:S(2)}, u32[]{:S(2)}) collective-permute-start(bf16[256,512]{1,0:T(8,128)(2,1)S(1)} %copy.54), channel_id=1, source_target_pairs={{0,4},{1,12},{4,8},{5,0},{8,13},{9,5},{12,1},{13,9},{2,6},{3,14},{... | collective-permute-start | bytes 786440 | tf_op jit(solution)/shard_map/return_heads/ppermute | solution.py:47
  303.9 7.6 %collective-permute-start.11 = (bf16[256,512]{1,0:T(8,128)(2,1)S(1)}, bf16[256,512]{1,0:T(8,128)(2,1)S(1)}, u32[]{:S(2)}, u32[]{:S(2)}) collective-permute-start(bf16[256,512]{1,0:T(8,128)(2,1)S(1)} %copy.53), channel_id=1, source_target_pairs={{0,0},{1,8},{4,4},{5,12},{8,9},{9,1},{12,13},{13,5},{2,2},{3,10},{... | collective-permute-start | bytes 786440 | tf_op jit(solution)/shard_map/return_heads/ppermute | solution.py:47
  305.2 14.2 %all-to-all-start.6 = ((f32[4,2,2048]{2,1,0:T(2,128)}), f32[4,2,2048]{2,1,0:T(2,128)S(1)}, u32[]{:S(2)}, u32[]{:S(2)}) async-start(f32[4,2,2048]{2,1,0:T(2,128)} %broadcast_in_dim.28), calls=%async_computation.6 | async-start | bytes 131072 | tf_op jit(solution)/shard_map/direction/all_to_all | solution.py:35
  320.4 32.2 %all-to-all-start.4 = ((f32[64,2,1024]{2,1,0:T(2,128)}), f32[64,2,1024]{2,1,0:T(2,128)S(1)}, u32[]{:S(2)}, u32[]{:S(2)}) async-start(f32[64,2,1024]{2,1,0:T(2,128)} %broadcast_in_dim.26), calls=%async_computation.4 | async-start | bytes 1048576 | tf_op jit(solution)/shard_map/tail/all_to_all | solution.py:35
  352.6 15.2 %all-to-all-start.7 = ((f32[64,2,128]{2,1,0:T(2,128)}), f32[64,2,128]{2,1,0:T(2,128)S(1)}, u32[]{:S(2)}, u32[]{:S(2)}) async-start(f32[64,2,128]{2,1,0:T(2,128)} %copy.57), calls=%async_computation.7 | async-start | bytes 131072 | tf_op jit(solution)/shard_map/direction/all_to_all | solution.py:106
  368.4 11.8 %all-to-all-start.9 = ((f32[4,64,128]{2,1,0:T(8,128)}), f32[4,64,128]{2,1,0:T(8,128)S(1)}, u32[]{:S(2)}, u32[]{:S(2)}) async-start(f32[4,64,128]{2,1,0:T(8,128)} %broadcast_in_dim.30), calls=%async_computation.9 | async-start | bytes 262144 | tf_op jit(solution)/shard_map/tail/all_to_all | solution.py:35
  380.3 18.1 %all-to-all-start.8 = ((f32[64,1,1024]{2,1,0:T(1,128)}), f32[64,1,1024]{2,1,0:T(1,128)S(1)}, u32[]{:S(2)}, u32[]{:S(2)}) async-start(f32[64,1,1024]{2,1,0:T(1,128)} %copy.59), calls=%async_computation.8 | async-start | bytes 524288 | tf_op jit(solution)/shard_map/direction/all_to_all | solution.py:111
  398.4 17.8 %all-to-all-start.10 = ((f32[64,1,1152]{2,1,0:T(1,128)}), f32[64,1,1152]{2,1,0:T(1,128)S(1)}, u32[]{:S(2)}, u32[]{:S(2)}) async-start(f32[64,1,1152]{2,1,0:T(1,128)} %copy.62), calls=%async_computation.10 | async-start | bytes 589824 | tf_op jit(solution)/shard_map/tail/all_to_all | solution.py:161
  (13 other events, 30.8 us)
Sparse Core Ops, SparseCore 0:
  18.0 54.5 all-gather.2
